TPU v7x, 32 devices: a whole 2x2x4 slice. The times are simulated.
32 devices in a mesh: leaf: 4 (over y, x), front: 8 (over z, core).
Axes of the slice: x: 2, y: 2, z: 4, core: 2. Of those that a mesh axis runs over, the one named last changes fastest.
Arguments:
- factored_panel: bfloat16 [4096, 1536], P(('leaf', 'front')), may hold values from -2.5 to 2.5
- front_tiles: float32 [256, 128, 128], P(('leaf', 'front')), may hold values from -6 to 6
- ancestor_tiles: float32 [256, 128, 128], P(('leaf', 'front')), may hold values from -6 to 6
- send_slots: int32 [32, 8], P(('leaf', 'front')), may hold values from -1 to 3, as said below
- extend_slots: int32 [32, 4], P(('leaf', 'front')), may hold values from 0 to 7
Outputs:
- assembled: float32 [256, 128, 128], P(('leaf', 'front'))
Inputs may be any that keep to these rules, and one draw needn't show every extreme that they name: `send_slots`: A value of -1 marks a block row without a tile; any other value is d + p, a leaf group d and a position p, and the values other than -1 in one row are distinct. In every leaf group the row of front index 0 uses all 4 values.
All inputs are finite; a program needn't handle non-finite values.
Results may differ from a plain program's by a relative error of at most 0.0003.
Values may be sent and summed in bfloat16 or wider, within the bound.
A program may use at most 64 MiB of HBM per device.

v0:
```python
import jax
import jax.numpy as jnp
from jax import lax
from jax.sharding import PartitionSpec as P

CAP = 1


def shards(factored_panel, front_tiles, ancestor_tiles, send_slots, extend_slots):
    leaf_count = lax.axis_size("leaf")
    message_slots = leaf_count * CAP
    blocks = front_tiles.shape[0]
    tile_size = front_tiles.shape[1]
    targets = send_slots[0]
    wanted = (targets[None, :] == jnp.arange(message_slots, dtype=jnp.int32)[:, None]).astype(
        jnp.int32
    )
    source_row = jnp.sum(wanted * jnp.arange(blocks, dtype=jnp.int32)[None, :], axis=1)
    present = jnp.sum(wanted, axis=1).astype(jnp.float32)[:, None, None]
    column = jnp.einsum(
        "rk,ck->rc",
        lax.all_gather(factored_panel, "front", axis=0, tiled=True),
        factored_panel,
        preferred_element_type=jnp.float32,
    )
    schur_tiles = front_tiles - column.reshape(blocks, tile_size, tile_size)
    message = jnp.take(schur_tiles, source_row, axis=0) * present
    outgoing = message.reshape(leaf_count, CAP, tile_size, tile_size)
    incoming = lax.all_to_all(outgoing, "leaf", split_axis=0, concat_axis=0, tiled=True)
    received = incoming.reshape(message_slots, tile_size * tile_size)
    held_tiles = ancestor_tiles.shape[0]
    target_table = (
        extend_slots[0][None, :] == jnp.arange(held_tiles, dtype=jnp.int32)[:, None]
    ).astype(jnp.float32)
    extended = jnp.dot(
        target_table, received, precision=lax.Precision.HIGHEST, preferred_element_type=jnp.float32
    )
    return ancestor_tiles + extended.reshape(held_tiles, tile_size, tile_size)


def solution(mesh):
    placed = (
        P(("leaf", "front"), None),
        P(("leaf", "front"), None, None),
        P(("leaf", "front"), None, None),
        P(("leaf", "front"), None),
        P(("leaf", "front"), None),
    )
    return jax.shard_map(
        shards,
        mesh=mesh,
        in_specs=placed,
        out_specs=P(("leaf", "front"), None, None),
        check_vma=False,
    )
```

profile of v0, /device:TPU:0, one launch (start us, length us, event | category | flops | bytes accessed | tf_op | source)
XLA Modules:
  0.0 71.8 jit_solution(15475049399767781264)
XLA Ops:
  6.5 0.0 copy-start
  6.5 0.0 all-gather.2.cloned.1.call-start
  6.5 0.7 all-gather.2.cloned.1.call-update
  7.3 0.8 %convert_reduce_fusion = (s32[4]{0:T(128)S(1)}, s32[4]{0:T(128)S(1)}) fusion(s32[8]{0:T(128)} %bitcast.29), kind=kLoop, calls=%fused_computation.9 | loop fusion | flops 152 | bytes 64 | tf_op jit(solution)/shard_map/reduce_sum | solution.py:19
  8.1 0.0 copy-start.1
  8.1 0.0 copy-start.2
  8.1 41.9 %all-gather.2.cloned.1.call-done = bf16[1024,1536]{1,0:T(8,128)(2,1)} async-done(((bf16[128,1536]{1,0:T(8,128)(2,1)}), bf16[1024,1536]{1,0:T(8,128)(2,1)}) %all-gather.2.cloned.1.call-update) | async-done | bytes 3145744 | tf_op jit(solution)/shard_map/all_gather | solution.py:22
  50.0 2.9 %fusion.6 = f32[1024,128]{1,0:T(8,128)S(1)} fusion(bf16[1024,1536]{1,0:T(8,128)(2,1)} %all-gather.2.cloned.1.call-done, bf16[128,1536]{1,0:T(8,128)(2,1)} %param.5), kind=kOutput, calls=%fused_computation.17 | convolution fusion | flops 402653184 | bytes 4063232 | tf_op jit(solution)/shard_map/rk,ck->rc/dot_general | solution.py:20
  52.9 0.0 copy-done
  52.9 0.1 sub.3
  53.0 0.6 gather_fusion
  53.6 0.1 fusion.1
  53.7 9.6 %all_to_all.5 = f32[4,1,128,128]{3,2,1,0:T(8,128)S(1)} all-to-all(f32[4,1,128,128]{3,2,1,0:T(8,128)S(1)} %fusion.1), channel_id=1, replica_groups=mesh['leaf'=4,'front'=8] {'leaf'}, dimensions={0} | all-to-all | bytes 524288 | tf_op jit(solution)/shard_map/all_to_all | solution.py:29
  63.2 0.0 copy-done.1
  63.2 0.0 copy-done.2
  63.2 0.8 %convolution_add_fusion = f32[8,128,128]{2,0,1:T(8,128)S(1)} fusion(f32[8,128,128]{2,1,0:T(8,128)S(1)} %copy-done.1, f32[1,4,128,128]{3,2,1,0:T(8,128)S(1)} %bitcast.27, s32[4]{0:T(128)S(1)} %bitcast.28), kind=kOutput, calls=%fused_computation.1 | convolution fusion | flops 6422560 | bytes 1310736 | tf_op jit(solution)/shard_map/dot_general | solution.py:35
  64.1 0.9 %copy.11 = f32[8,128,128]{2,1,0:T(8,128)} copy(f32[8,128,128]{2,0,1:T(8,128)S(1)} %convolution_add_fusion) | data formatting | bytes 1048576 | tf_op jit(solution)/shard_map/add | solution.py:38
  (4 shorter events, 0.0 us)
Async XLA Ops:
  6.5 46.4 %copy-start = (f32[8,128,128]{2,1,0:T(8,128)S(1)}, f32[8,128,128]{2,1,0:T(8,128)}, u32[]{:S(2)}) copy-start(f32[8,128,128]{2,1,0:T(8,128)} %param.6) | copy-start | bytes 1572868
  6.5 43.5 %all-gather.2.cloned.1.call-start = ((), (), s32[]{:S(2)}) async-start(), calls=%async_computation.1 | async-start | bytes 3538944 | tf_op jit(solution)/shard_map/all_gather | solution.py:22
  8.1 55.1 %copy-start.1 = (f32[8,128,128]{2,1,0:T(8,128)S(1)}, f32[8,128,128]{2,1,0:T(8,128)}, u32[]{:S(2)}) copy-start(f32[8,128,128]{2,1,0:T(8,128)} %param.7) | copy-start | bytes 1572868
  8.1 55.1 %copy-start.2 = (s32[1,4]{1,0:T(1,128)S(1)}, s32[1,4]{1,0:T(1,128)}, u32[]{:S(2)}) copy-start(s32[1,4]{1,0:T(1,128)} %param.9) | copy-start | bytes 52
Sparse Core Ops, SparseCore 0:
  9.0 40.9 all-gather.1
where the time goes:
time: 72 us; the launch traced here: 71.8 us
  waiting for transfers between devices  42.6 us (59%)
  between operations  13.5 us (19%)
  blocking collectives  9.56 us (13%)
  matrix products  3.75 us (5%)
  local copies, waits for them, and re-layouts  1.47 us (2%)
  other arithmetic  0.98 us (1%)
    all_gather x1, waiting for transfers between devices, shards(): lax.all_gather(factored_panel, 'front', axis=0, tiled=True)  41.9 us
    all_to_all x1, blocking collectives, shards(): lax.all_to_all(outgoing, 'leaf', split_axis=0, concat_axis=0, tiled=True)  9.56 us
    dot_general x1, matrix products, shards(): jnp.einsum('rk,ck->rc', lax.all_gather(factored_panel, 'front', axis=0, t...  2.91 us
  transfers between devices with their start and end apart: 1, of which 1 were waited for; matrix products, arithmetic and copies ran while one was open for 1% of the time, Pallas kernels for 0%

commit v1 on v0

v1 whole, which is shorter than its diff:
```python
import functools

import jax
import jax.numpy as jnp
from jax import lax
from jax.experimental import pallas as pl
from jax.experimental.pallas import tpu as pltpu
from jax.sharding import PartitionSpec as P

MESH = pl.DeviceIdType.MESH
UP, DOWN, SIDE = 0, 1, 2


def kernel(nz, n_leaf, chunks, panel, front, ancestor, targets, extend, out,
           held, schur, message, received, send_sem, recv_sem, leaf_send, leaf_recv):
    leaf = lax.axis_index("leaf")
    f = lax.axis_index("front")
    z, c = f // 2, f % 2
    side = f + 1 - 2 * c
    below, above = z > 0, z < nz - 1
    rows = panel.shape[0] // chunks
    blocks = schur.shape[0]

    barrier = pltpu.get_barrier_semaphore()

    def greet(device):
        pl.semaphore_signal(barrier, inc=1, device_id=device, device_id_type=MESH)

    pl.when(below)(lambda: greet((leaf, f - 2)))
    pl.when(above)(lambda: greet((leaf, f + 2)))
    greet((leaf, side))
    for j in range(1, n_leaf):
        greet(((leaf + j) % n_leaf, f))
    pl.semaphore_wait(
        barrier, n_leaf + below.astype(jnp.int32) + above.astype(jnp.int32)
    )

    def piece(ref, k):
        return ref.at[pl.ds(k * rows, rows)]

    def copy(way, source, block, k):
        to = {UP: f + 2, DOWN: f - 2, SIDE: side}[way]
        return pltpu.make_async_remote_copy(
            src_ref=piece(source, k),
            dst_ref=piece(held.at[block], k),
            send_sem=send_sem.at[way, block, k],
            recv_sem=recv_sem.at[block, k],
            device_id=(leaf, to),
            device_id_type=MESH,
        )

    def arrived(block, k):
        copy(SIDE, held.at[block], block, k).wait_recv()

    def product(source, block):
        schur[block] = front[block] - lax.dot_general(
            source[...], panel[...], (((1,), (1,)), ((), ())),
            preferred_element_type=jnp.float32,
        )

    for k in range(chunks):
        pl.when(above)(lambda: copy(UP, panel, f, k).start())
        pl.when(below)(lambda: copy(DOWN, panel, f, k).start())
    for k in range(chunks):
        copy(SIDE, panel, f, k).start()
    product(panel, f)
    for k in range(chunks):
        arrived(side, k)
    product(held.at[side], side)

    def step(s, carry):
        lo, hi = z - 1 - s, z + 1 + s
        for k in range(chunks):
            @pl.when(lo >= 0)
            def _():
                b = lo * 2 + c
                arrived(b, k)
                pl.when(above)(lambda: copy(UP, held.at[b], b, k).start())
                copy(SIDE, held.at[b], b, k).start()

            @pl.when(hi < nz)
            def _():
                b = hi * 2 + c
                arrived(b, k)
                pl.when(below)(lambda: copy(DOWN, held.at[b], b, k).start())
                copy(SIDE, held.at[b], b, k).start()

        for far, there in ((lo, lo >= 0), (hi, hi < nz)):
            @pl.when(there)
            def _():
                product(held.at[far * 2 + c], far * 2 + c)

        for far, there in ((lo, lo >= 0), (hi, hi < nz)):
            @pl.when(there)
            def _():
                b = far * 2 + 1 - c
                for k in range(chunks):
                    arrived(b, k)
                product(held.at[b], b)
        return carry

    lax.fori_loop(0, nz - 1, step, 0)

    def pick(d):
        row, present = jnp.int32(0), jnp.int32(0)
        for i in range(blocks):
            hit = targets[0, i] == d
            row = jnp.where(hit, i, row)
            present = jnp.where(hit, 1, present)
        tile = schur[row]
        return jnp.where(present > 0, tile, jnp.zeros_like(tile))

    def leaf_copy(j):
        return pltpu.make_async_remote_copy(
            src_ref=message.at[j],
            dst_ref=received.at[leaf],
            send_sem=leaf_send.at[j],
            recv_sem=leaf_recv.at[leaf],
            device_id=((leaf + j) % n_leaf, f),
            device_id_type=MESH,
        )

    for j in range(1, n_leaf):
        message[j] = pick((leaf + j) % n_leaf)
        leaf_copy(j).start()
    received[leaf] = pick(leaf)

    def settle(block, forwards_up, forwards_down):
        for k in range(chunks):
            pl.when(forwards_up)(lambda: copy(UP, panel, block, k).wait_send())
            pl.when(forwards_down)(lambda: copy(DOWN, panel, block, k).wait_send())
            copy(SIDE, panel, block, k).wait_send()

    settle(f, above, below)

    def settle_step(s, carry):
        lo, hi = z - 1 - s, z + 1 + s
        pl.when(lo >= 0)(lambda: settle(lo * 2 + c, above, False))
        pl.when(hi < nz)(lambda: settle(hi * 2 + c, False, below))
        return carry

    lax.fori_loop(0, nz - 1, settle_step, 0)

    for j in range(1, n_leaf):
        g = (leaf + n_leaf - j) % n_leaf
        pltpu.make_async_remote_copy(
            src_ref=message.at[j],
            dst_ref=received.at[g],
            send_sem=leaf_send.at[j],
            recv_sem=leaf_recv.at[g],
            device_id=((leaf + j) % n_leaf, f),
            device_id_type=MESH,
        ).wait_recv()
    for a in range(out.shape[0]):
        total = ancestor[a]
        for g in range(n_leaf):
            tile = received[g]
            total = total + jnp.where(extend[0, g] == a, tile, jnp.zeros_like(tile))
        out[a] = total
    for j in range(1, n_leaf):
        leaf_copy(j).wait_send()


def shards(factored_panel, front_tiles, ancestor_tiles, send_slots, extend_slots):
    n_leaf = lax.axis_size("leaf")
    n_front = lax.axis_size("front")
    nz = n_front // 2
    chunks = max(1, 16 // nz)
    blocks, tile_size = front_tiles.shape[0], front_tiles.shape[1]
    rows, width = factored_panel.shape
    vmem = pl.BlockSpec(memory_space=pltpu.VMEM)
    smem = pl.BlockSpec(memory_space=pltpu.SMEM)
    return pl.pallas_call(
        functools.partial(kernel, nz, n_leaf, chunks),
        out_shape=jax.ShapeDtypeStruct(ancestor_tiles.shape, jnp.float32),
        in_specs=[vmem, vmem, vmem, smem, smem],
        out_specs=vmem,
        scratch_shapes=[
            pltpu.VMEM((n_front, rows, width), jnp.bfloat16),
            pltpu.VMEM((blocks, tile_size, tile_size), jnp.float32),
            pltpu.VMEM((n_leaf, tile_size, tile_size), jnp.float32),
            pltpu.VMEM((n_leaf, tile_size, tile_size), jnp.float32),
            pltpu.SemaphoreType.DMA((3, n_front, chunks)),
            pltpu.SemaphoreType.DMA((n_front, chunks)),
            pltpu.SemaphoreType.DMA((n_leaf,)),
            pltpu.SemaphoreType.DMA((n_leaf,)),
        ],
        compiler_params=pltpu.CompilerParams(
            collective_id=0, has_side_effects=True, vmem_limit_bytes=40 * 1024 * 1024
        ),
        cost_estimate=pl.CostEstimate(
            flops=2 * blocks * tile_size * rows * width,
            bytes_accessed=2 * n_front * rows * width,
            transcendentals=0,
        ),
    )(factored_panel, front_tiles, ancestor_tiles, send_slots, extend_slots)


def solution(mesh):
    placed = (
        P(("leaf", "front"), None),
        P(("leaf", "front"), None, None),
        P(("leaf", "front"), None, None),
        P(("leaf", "front"), None),
        P(("leaf", "front"), None),
    )
    return jax.shard_map(
        shards,
        mesh=mesh,
        in_specs=placed,
        out_specs=P(("leaf", "front"), None, None),
        check_vma=False,
    )
```

time: 72 us -> 43.8 us (0.61)
  waiting for transfers between devices: 42.6 us -> 0 us
  Pallas kernels: 0 us -> 38.3 us
  between operations: 13.5 us -> 0.01 us
  blocking collectives: 9.56 us -> 0 us
  matrix products: 3.75 us -> 0 us
  local copies, waits for them, and re-layouts: 1.47 us -> 5.18 us
  other arithmetic: 0.98 us -> 0 us
    all_gather x1 -> x0, waiting for transfers between devices: 41.9 us -> none  [shards(): lax.all_gather(factored_panel, 'front', axis=0, tiled=True)]
    pallas_call x0 -> x1, Pallas kernels: none -> 38.3 us  [shards(): pl.pallas_call(functools.partial(kernel, nz, n_leaf, chunks), out_shape=j...]
    all_to_all x1 -> x0, blocking collectives: 9.56 us -> none  [shards(): lax.all_to_all(outgoing, 'leaf', split_axis=0, concat_axis=0, tiled=True)]
    unnamed x6 -> x11, local copies, waits for them, and re-layouts: 0.02 us -> 5.18 us
    dot_general x2 -> x0, matrix products: 3.75 us -> none  [the longest x1 2.91 us: shards(): jnp.einsum('rk,ck->rc', lax.all_gather(factored_panel, 'front', axis=0, t...]
    add x1 -> x0, local copies, waits for them, and re-layouts: 0.89 us -> none  [shards(): return ancestor_tiles + extended.reshape(held_tiles, tile_size, tile_size)]
    reduce_sum x1 -> x0, other arithmetic: 0.8 us -> none  [shards(): present = jnp.sum(wanted, axis=1).astype(jnp.float32)[:, None, None]]
  transfers between devices with their start and end apart: 1 -> 0, of which waited for: 1 -> 0; matrix products, arithmetic and copies ran while one was open for 1% -> 0% of each run, Pallas kernels for 0% -> 0%
where the time goes in v1:
time: 43.8 us; the launch traced here: 43.5 us
  Pallas kernels  38.3 us (87%)
  local copies, waits for them, and re-layouts  5.18 us (12%)
    pallas_call x1, Pallas kernels, shards(): pl.pallas_call(functools.partial(kernel, nz, n_leaf, chunks), out_shape=j...  38.3 us
    unnamed x11, local copies, waits for them, and re-layouts  5.18 us

profile of v1, /device:TPU:0, one launch (start us, length us, event | category | flops | bytes accessed | tf_op | source)
XLA Modules:
  0.0 43.5 jit_solution(2952197390502260979)
XLA Ops:
  0.0 0.0 copy-start
  0.0 1.0 %copy-done = f32[8,128,128]{2,1,0:T(8,128)S(1)} copy-done((f32[8,128,128]{2,1,0:T(8,128)S(1)}, f32[8,128,128]{2,1,0:T(8,128)}, u32[]{:S(2)}) %copy-start) | copy-done | bytes 524312
  1.0 0.0 copy-start.1
  1.0 1.0 %copy-done.1 = f32[8,128,128]{2,1,0:T(8,128)S(1)} copy-done((f32[8,128,128]{2,1,0:T(8,128)S(1)}, f32[8,128,128]{2,1,0:T(8,128)}, u32[]{:S(2)}) %copy-start.1) | copy-done | bytes 524312
  2.1 0.0 copy-start.2
  2.1 1.0 %copy-done.2 = bf16[128,1536]{1,0:T(8,128)(2,1)S(1)} copy-done((bf16[128,1536]{1,0:T(8,128)(2,1)S(1)}, bf16[128,1536]{1,0:T(8,128)(2,1)}, u32[]{:S(2)}) %copy-start.2) | copy-done | bytes 393240
  3.1 0.0 copy-start.3
  3.1 0.7 %copy-done.3 = s32[1,8]{1,0:T(1,128)S(1)} copy-done((s32[1,8]{1,0:T(1,128)S(1)}, s32[1,8]{1,0:T(1,128)}, u32[]{:S(2)}) %copy-start.3) | copy-done | bytes 56
  3.7 0.0 copy-start.4
  3.7 0.7 %copy-done.4 = s32[1,4]{1,0:T(1,128)S(1)} copy-done((s32[1,4]{1,0:T(1,128)S(1)}, s32[1,4]{1,0:T(1,128)}, u32[]{:S(2)}) %copy-start.4) | copy-done | bytes 40
  4.4 38.3 %shard_map.55 = f32[8,128,128]{2,1,0:T(8,128)S(1)} custom-call(bf16[128,1536]{1,0:T(8,128)(2,1)S(1)} %copy-done.2, f32[8,128,128]{2,1,0:T(8,128)S(1)} %copy-done, f32[8,128,128]{2,1,0:T(8,128)S(1)} %copy-done.1, s32[1,8]{1,0:T(1,128)S(1)} %copy-done.3, s32[1,4]{1,0:T(1,128)S(1)} %copy-done.4), custom_call_target="tpu_custom_call" | custom-call | flops 402653184 | bytes 3145728 | tf_op jit(solution)/shard_map/pallas_call | solution.py:173
  42.7 0.8 %copy.7 = f32[8,128,128]{2,1,0:T(8,128)} copy(f32[8,128,128]{2,1,0:T(8,128)S(1)} %shard_map.55) | data formatting | bytes 1048576
Async XLA Ops:
  0.0 1.0 %copy-start = (f32[8,128,128]{2,1,0:T(8,128)S(1)}, f32[8,128,128]{2,1,0:T(8,128)}, u32[]{:S(2)}) copy-start(f32[8,128,128]{2,1,0:T(8,128)} %front.1) | copy-start | bytes 1572868
  1.0 1.0 %copy-start.1 = (f32[8,128,128]{2,1,0:T(8,128)S(1)}, f32[8,128,128]{2,1,0:T(8,128)}, u32[]{:S(2)}) copy-start(f32[8,128,128]{2,1,0:T(8,128)} %ancestor.1) | copy-start | bytes 1572868
  2.1 1.0 %copy-start.2 = (bf16[128,1536]{1,0:T(8,128)(2,1)S(1)}, bf16[128,1536]{1,0:T(8,128)(2,1)}, u32[]{:S(2)}) copy-start(bf16[128,1536]{1,0:T(8,128)(2,1)} %panel.1) | copy-start | bytes 1179652
  3.1 0.7 %copy-start.3 = (s32[1,8]{1,0:T(1,128)S(1)}, s32[1,8]{1,0:T(1,128)}, u32[]{:S(2)}) copy-start(s32[1,8]{1,0:T(1,128)} %targets.1) | copy-start | bytes 100
  3.7 0.7 %copy-start.4 = (s32[1,4]{1,0:T(1,128)S(1)}, s32[1,4]{1,0:T(1,128)}, u32[]{:S(2)}) copy-start(s32[1,4]{1,0:T(1,128)} %extend.1) | copy-start | bytes 52

commit v2 on v1

--- a/solution.py
+++ b/solution.py
@@ -9,17 +9,30 @@
 
 MESH = pl.DeviceIdType.MESH
 UP, DOWN, SIDE = 0, 1, 2
-
-
-def kernel(nz, n_leaf, chunks, panel, front, ancestor, targets, extend, out,
-           held, schur, message, received, send_sem, recv_sem, leaf_send, leaf_recv):
+ACROSS, MATE = 0, 1
+
+
+def kernel(nz, n_leaf, chunks, panel_hbm, front_hbm, ancestor_hbm, targets_hbm, extend_hbm, out,
+           pair, front, ancestor, targets, extend, held, schur, made, taken, message, received,
+           load_sem, send_sem, recv_sem, tile_send, tile_recv, leaf_send, leaf_recv):
     leaf = lax.axis_index("leaf")
     f = lax.axis_index("front")
     z, c = f // 2, f % 2
     side = f + 1 - 2 * c
     below, above = z > 0, z < nz - 1
-    rows = panel.shape[0] // chunks
+    size = panel_hbm.shape[0]
+    rows = size // chunks
     blocks = schur.shape[0]
+    panel = pair.at[pl.ds(0, size)]
+    loads = [
+        pltpu.make_async_copy(source, to, load_sem.at[n])
+        for n, (source, to) in enumerate((
+            (panel_hbm, panel), (front_hbm, front), (ancestor_hbm, ancestor),
+            (targets_hbm, targets), (extend_hbm, extend),
+        ))
+    ]
+    for load in loads:
+        load.start()
 
     barrier = pltpu.get_barrier_semaphore()
 
@@ -58,48 +71,200 @@
             preferred_element_type=jnp.float32,
         )
 
-    for k in range(chunks):
-        pl.when(above)(lambda: copy(UP, panel, f, k).start())
-        pl.when(below)(lambda: copy(DOWN, panel, f, k).start())
-    for k in range(chunks):
-        copy(SIDE, panel, f, k).start()
-    product(panel, f)
-    for k in range(chunks):
-        arrived(side, k)
-    product(held.at[side], side)
-
-    def step(s, carry):
-        lo, hi = z - 1 - s, z + 1 + s
-        for k in range(chunks):
-            @pl.when(lo >= 0)
-            def _():
-                b = lo * 2 + c
-                arrived(b, k)
-                pl.when(above)(lambda: copy(UP, held.at[b], b, k).start())
-                copy(SIDE, held.at[b], b, k).start()
-
-            @pl.when(hi < nz)
-            def _():
-                b = hi * 2 + c
-                arrived(b, k)
-                pl.when(below)(lambda: copy(DOWN, held.at[b], b, k).start())
-                copy(SIDE, held.at[b], b, k).start()
-
-        for far, there in ((lo, lo >= 0), (hi, hi < nz)):
-            @pl.when(there)
-            def _():
-                product(held.at[far * 2 + c], far * 2 + c)
-
-        for far, there in ((lo, lo >= 0), (hi, hi < nz)):
-            @pl.when(there)
-            def _():
-                b = far * 2 + 1 - c
-                for k in range(chunks):
+    loads[0].wait()
+    loads[1].wait()
+
+    def relay():
+        for k in range(chunks):
+            pl.when(above)(lambda: copy(UP, panel, f, k).start())
+            pl.when(below)(lambda: copy(DOWN, panel, f, k).start())
+        for k in range(chunks):
+            copy(SIDE, panel, f, k).start()
+        product(panel, f)
+        for k in range(chunks):
+            arrived(side, k)
+        product(held.at[side], side)
+
+        def step(s, carry):
+            lo, hi = z - 1 - s, z + 1 + s
+            for k in range(chunks):
+                @pl.when(lo >= 0)
+                def _():
+                    b = lo * 2 + c
                     arrived(b, k)
-                product(held.at[b], b)
-        return carry
-
-    lax.fori_loop(0, nz - 1, step, 0)
+                    pl.when(above)(lambda: copy(UP, held.at[b], b, k).start())
+                    copy(SIDE, held.at[b], b, k).start()
+
+                @pl.when(hi < nz)
+                def _():
+                    b = hi * 2 + c
+                    arrived(b, k)
+                    pl.when(below)(lambda: copy(DOWN, held.at[b], b, k).start())
+                    copy(SIDE, held.at[b], b, k).start()
+
+            for far, there in ((lo, lo >= 0), (hi, hi < nz)):
+                @pl.when(there)
+                def _():
+                    product(held.at[far * 2 + c], far * 2 + c)
+
+            for far, there in ((lo, lo >= 0), (hi, hi < nz)):
+                @pl.when(there)
+                def _():
+                    b = far * 2 + 1 - c
+                    for k in range(chunks):
+                        arrived(b, k)
+                    product(held.at[b], b)
+            return carry
+
+        lax.fori_loop(0, nz - 1, step, 0)
+
+    def relay_settle():
+        def settle(block, forwards_up, forwards_down):
+            for k in range(chunks):
+                pl.when(forwards_up)(lambda: copy(UP, panel, block, k).wait_send())
+                pl.when(forwards_down)(lambda: copy(DOWN, panel, block, k).wait_send())
+                copy(SIDE, panel, block, k).wait_send()
+
+        settle(f, above, below)
+
+        def settle_step(s, carry):
+            lo, hi = z - 1 - s, z + 1 + s
+            pl.when(lo >= 0)(lambda: settle(lo * 2 + c, above, False))
+            pl.when(hi < nz)(lambda: settle(hi * 2 + c, False, below))
+            return carry
+
+        lax.fori_loop(0, nz - 1, settle_step, 0)
+
+    mate, across = z + 1 - 2 * (z % 2), nz - 1 - z
+    inner = (z > 0) & (z < nz - 1)
+    pieces = 2
+    tall = size // pieces
+
+    def pass_on(way, source, block, k):
+        to = {ACROSS: across * 2 + c, MATE: mate * 2 + c, SIDE: side}[way]
+        return pltpu.make_async_remote_copy(
+            src_ref=piece(source, k),
+            dst_ref=piece(held.at[block], k),
+            send_sem=send_sem.at[way, block, k],
+            recv_sem=recv_sem.at[block, k],
+            device_id=(leaf, to),
+            device_id_type=MESH,
+        )
+
+    def tile_copy(block, n):
+        return pltpu.make_async_remote_copy(
+            src_ref=made.at[block, pl.ds(n * tall, tall)],
+            dst_ref=taken.at[block, pl.ds(n * tall, tall)],
+            send_sem=tile_send.at[block, n],
+            recv_sem=tile_recv.at[block, n],
+            device_id=(leaf, mate * 2 + c),
+            device_id_type=MESH,
+        )
+
+    def both(block, n):
+        at = pl.ds(n * tall, tall)
+        result = lax.dot_general(
+            held[block, at], pair[...], (((1,), (1,)), ((), ())),
+            preferred_element_type=jnp.float32,
+        )
+        made[block, at] = result[:, size:]
+        tile_copy(block, n).start()
+        schur[block, at] = front[block, at] - result[:, :size]
+
+    far_inner, far_outer = across, nz - 1 - mate
+
+    def inner_start():
+        for k in range(chunks):
+            pass_on(ACROSS, panel, f, k).start()
+            pass_on(MATE, panel, f, k).start()
+        for k in range(chunks):
+            pass_on(SIDE, panel, f, k).start()
+        product(panel, f)
+        for k in range(chunks):
+            arrived(side, k)
+        product(held.at[side], side)
+        near, far = mate * 2 + c, far_inner * 2 + c
+        for k in range(chunks):
+            arrived(near, k)
+            pass_on(ACROSS, held.at[near], near, k).start()
+            pass_on(SIDE, held.at[near], near, k).start()
+            arrived(far, k)
+            pass_on(SIDE, held.at[far], far, k).start()
+        pair[pl.ds(size, size)] = held[near]
+        for n in range(pieces):
+            both(far, n)
+        far = far_inner * 2 + 1 - c
+        for k in range(chunks):
+            arrived(far, k)
+        for n in range(pieces):
+            both(far, n)
+        product(held.at[near], near)
+        near = mate * 2 + 1 - c
+        for k in range(chunks):
+            arrived(near, k)
+        product(held.at[near], near)
+        far, other = far_outer * 2 + c, far_outer * 2 + 1 - c
+        for n in range(pieces):
+            part = range(n * chunks // pieces, (n + 1) * chunks // pieces)
+            for k in part:
+                arrived(far, k)
+                pass_on(SIDE, held.at[far], far, k).start()
+            both(far, n)
+            for k in part:
+                arrived(other, k)
+            both(other, n)
+
+    def outer_start():
+        for k in range(chunks):
+            pass_on(MATE, panel, f, k).start()
+        for k in range(chunks):
+            pass_on(SIDE, panel, f, k).start()
+        product(panel, f)
+        for k in range(chunks):
+            arrived(side, k)
+        product(held.at[side], side)
+        near, other = mate * 2 + c, mate * 2 + 1 - c
+        for k in range(chunks):
+            arrived(near, k)
+            pass_on(SIDE, held.at[near], near, k).start()
+        product(held.at[near], near)
+        for k in range(chunks):
+            arrived(other, k)
+        product(held.at[other], other)
+        for there in (far_outer, far_inner):
+            for n in range(pieces):
+                at = pl.ds(n * tall, tall)
+                for b in (there * 2 + c, there * 2 + 1 - c):
+                    tile_copy(b, n).wait_recv()
+                    schur[b, at] = front[b, at] - taken[b, at]
+
+    def inner_settle():
+        for k in range(chunks):
+            for way in (ACROSS, MATE, SIDE):
+                pass_on(way, panel, f, k).wait_send()
+            for way in (ACROSS, SIDE):
+                pass_on(way, panel, mate * 2 + c, k).wait_send()
+            pass_on(SIDE, panel, far_inner * 2 + c, k).wait_send()
+            pass_on(SIDE, panel, far_outer * 2 + c, k).wait_send()
+        for there in (far_outer, far_inner):
+            for n in range(pieces):
+                for b in (there * 2, there * 2 + 1):
+                    tile_copy(b, n).wait_send()
+
+    def outer_settle():
+        for k in range(chunks):
+            pass_on(MATE, panel, f, k).wait_send()
+            pass_on(SIDE, panel, f, k).wait_send()
+            pass_on(SIDE, panel, mate * 2 + c, k).wait_send()
+
+    halves = nz == 4
+    if halves:
+        pl.when(inner)(inner_start)
+        pl.when(jnp.logical_not(inner))(outer_start)
+    else:
+        relay()
+
+    loads[3].wait()
 
     def pick(d):
         row, present = jnp.int32(0), jnp.int32(0)
@@ -125,21 +290,13 @@
         leaf_copy(j).start()
     received[leaf] = pick(leaf)
 
-    def settle(block, forwards_up, forwards_down):
-        for k in range(chunks):
-            pl.when(forwards_up)(lambda: copy(UP, panel, block, k).wait_send())
-            pl.when(forwards_down)(lambda: copy(DOWN, panel, block, k).wait_send())
-            copy(SIDE, panel, block, k).wait_send()
-
-    settle(f, above, below)
-
-    def settle_step(s, carry):
-        lo, hi = z - 1 - s, z + 1 + s
-        pl.when(lo >= 0)(lambda: settle(lo * 2 + c, above, False))
-        pl.when(hi < nz)(lambda: settle(hi * 2 + c, False, below))
-        return carry
-
-    lax.fori_loop(0, nz - 1, settle_step, 0)
+    if halves:
+        pl.when(inner)(inner_settle)
+        pl.when(jnp.logical_not(inner))(outer_settle)
+    else:
+        relay_settle()
+    loads[2].wait()
+    loads[4].wait()
 
     for j in range(1, n_leaf):
         g = (leaf + n_leaf - j) % n_leaf
@@ -169,24 +326,34 @@
     blocks, tile_size = front_tiles.shape[0], front_tiles.shape[1]
     rows, width = factored_panel.shape
     vmem = pl.BlockSpec(memory_space=pltpu.VMEM)
-    smem = pl.BlockSpec(memory_space=pltpu.SMEM)
+    hbm = pl.BlockSpec(memory_space=pltpu.HBM)
     return pl.pallas_call(
         functools.partial(kernel, nz, n_leaf, chunks),
         out_shape=jax.ShapeDtypeStruct(ancestor_tiles.shape, jnp.float32),
-        in_specs=[vmem, vmem, vmem, smem, smem],
+        in_specs=[hbm] * 5,
         out_specs=vmem,
         scratch_shapes=[
+            pltpu.VMEM((2 * rows, width), jnp.bfloat16),
+            pltpu.VMEM(front_tiles.shape, jnp.float32),
+            pltpu.VMEM(ancestor_tiles.shape, jnp.float32),
+            pltpu.SMEM(send_slots.shape, jnp.int32),
+            pltpu.SMEM(extend_slots.shape, jnp.int32),
             pltpu.VMEM((n_front, rows, width), jnp.bfloat16),
+            pltpu.VMEM((blocks, tile_size, tile_size), jnp.float32),
+            pltpu.VMEM((blocks, tile_size, tile_size), jnp.float32),
             pltpu.VMEM((blocks, tile_size, tile_size), jnp.float32),
             pltpu.VMEM((n_leaf, tile_size, tile_size), jnp.float32),
             pltpu.VMEM((n_leaf, tile_size, tile_size), jnp.float32),
+            pltpu.SemaphoreType.DMA((5,)),
             pltpu.SemaphoreType.DMA((3, n_front, chunks)),
             pltpu.SemaphoreType.DMA((n_front, chunks)),
+            pltpu.SemaphoreType.DMA((blocks, 2)),
+            pltpu.SemaphoreType.DMA((blocks, 2)),
             pltpu.SemaphoreType.DMA((n_leaf,)),
             pltpu.SemaphoreType.DMA((n_leaf,)),
         ],
         compiler_params=pltpu.CompilerParams(
-            collective_id=0, has_side_effects=True, vmem_limit_bytes=40 * 1024 * 1024
+            collective_id=0, has_side_effects=True, vmem_limit_bytes=63 * 1024 * 1024
         ),
         cost_estimate=pl.CostEstimate(
             flops=2 * blocks * tile_size * rows * width,

time: 43.8 us -> 36.6 us (0.84)
  Pallas kernels: 38.3 us -> 34.5 us
  local copies, waits for them, and re-layouts: 5.18 us -> 1.87 us
    pallas_call x1, Pallas kernels: 38.3 us -> 34.5 us  [shards(): pl.pallas_call(functools.partial(kernel, nz, n_leaf, chunks), out_shape=j...]
    unnamed x11 -> x1, local copies, waits for them, and re-layouts: 5.18 us -> 1.87 us
where the time goes in v2:
time: 36.6 us; the launch traced here: 36.4 us
  Pallas kernels  34.5 us (94%)
  local copies, waits for them, and re-layouts  1.87 us (5%)
    pallas_call x1, Pallas kernels, shards(): pl.pallas_call(functools.partial(kernel, nz, n_leaf, chunks), out_shape=j...  34.5 us
    unnamed x1, local copies, waits for them, and re-layouts  1.87 us

profile of v2, /device:TPU:0, one launch (start us, length us, event | category | flops | bytes accessed | tf_op | source)
XLA Modules:
  0.0 36.4 jit_solution(3675598578047160457)
XLA Ops:
  0.0 34.5 %shard_map.55 = f32[8,128,128]{2,1,0:T(8,128)} custom-call(bf16[128,1536]{1,0:T(8,128)(2,1)} %panel_hbm.1, f32[8,128,128]{2,1,0:T(8,128)} %front_hbm.1, f32[8,128,128]{2,1,0:T(8,128)} %ancestor_hbm.1, s32[1,8]{1,0:T(1,128)} %targets_hbm.1, s32[1,4]{1,0:T(1,128)} %extend_hbm.1), custom_call_target="tpu_custom_call" | custom-call | flops 402653184 | bytes 3145728 | tf_op jit(solution)/shard_map/pallas_call | solution.py:330
  34.6 1.9 %copy.7 = f32[8,128,128]{2,1,0:T(8,128)} copy(f32[8,128,128]{2,1,0:T(8,128)} %shard_map.55) | data formatting | bytes 1048576

commit v3 on v2

--- a/solution.py
+++ b/solution.py
@@ -12,8 +12,8 @@
 ACROSS, MATE = 0, 1
 
 
-def kernel(nz, n_leaf, chunks, panel_hbm, front_hbm, ancestor_hbm, targets_hbm, extend_hbm, out,
-           pair, front, ancestor, targets, extend, held, schur, made, taken, message, received,
+def kernel(nz, n_leaf, chunks, panel_hbm, front_hbm, targets_hbm, received,
+           pair, front, targets, held, schur, made, taken, message,
            load_sem, send_sem, recv_sem, tile_send, tile_recv, leaf_send, leaf_recv):
     leaf = lax.axis_index("leaf")
     f = lax.axis_index("front")
@@ -27,8 +27,7 @@
     loads = [
         pltpu.make_async_copy(source, to, load_sem.at[n])
         for n, (source, to) in enumerate((
-            (panel_hbm, panel), (front_hbm, front), (ancestor_hbm, ancestor),
-            (targets_hbm, targets), (extend_hbm, extend),
+            (panel_hbm, panel), (front_hbm, front), (targets_hbm, targets),
         ))
     ]
     for load in loads:
@@ -176,9 +175,10 @@
     def inner_start():
         for k in range(chunks):
             pass_on(ACROSS, panel, f, k).start()
+        for k in range(chunks):
+            pass_on(SIDE, panel, f, k).start()
+        for k in range(chunks):
             pass_on(MATE, panel, f, k).start()
-        for k in range(chunks):
-            pass_on(SIDE, panel, f, k).start()
         product(panel, f)
         for k in range(chunks):
             arrived(side, k)
@@ -264,7 +264,7 @@
     else:
         relay()
 
-    loads[3].wait()
+    loads[2].wait()
 
     def pick(d):
         row, present = jnp.int32(0), jnp.int32(0)
@@ -288,16 +288,15 @@
     for j in range(1, n_leaf):
         message[j] = pick((leaf + j) % n_leaf)
         leaf_copy(j).start()
-    received[leaf] = pick(leaf)
+    message[0] = pick(leaf)
+    keep = pltpu.make_async_copy(message.at[0], received.at[leaf], leaf_recv.at[leaf])
+    keep.start()
 
     if halves:
         pl.when(inner)(inner_settle)
         pl.when(jnp.logical_not(inner))(outer_settle)
     else:
         relay_settle()
-    loads[2].wait()
-    loads[4].wait()
-
     for j in range(1, n_leaf):
         g = (leaf + n_leaf - j) % n_leaf
         pltpu.make_async_remote_copy(
@@ -308,43 +307,45 @@
             device_id=((leaf + j) % n_leaf, f),
             device_id_type=MESH,
         ).wait_recv()
-    for a in range(out.shape[0]):
-        total = ancestor[a]
-        for g in range(n_leaf):
-            tile = received[g]
-            total = total + jnp.where(extend[0, g] == a, tile, jnp.zeros_like(tile))
-        out[a] = total
+    keep.wait()
     for j in range(1, n_leaf):
         leaf_copy(j).wait_send()
+
+
+def extend_add(ancestor, received, extend, out):
+    first = pl.program_id(0) * out.shape[0]
+    out[...] = ancestor[...]
+    for g in range(received.shape[0]):
+        slot = extend[0, g] - first
+
+        @pl.when((slot >= 0) & (slot < out.shape[0]))
+        def _():
+            out[slot] += received[g]
 
 
 def shards(factored_panel, front_tiles, ancestor_tiles, send_slots, extend_slots):
     n_leaf = lax.axis_size("leaf")
     n_front = lax.axis_size("front")
     nz = n_front // 2
-    chunks = max(1, 16 // nz)
+    chunks = max(1, 8 // nz)
     blocks, tile_size = front_tiles.shape[0], front_tiles.shape[1]
     rows, width = factored_panel.shape
-    vmem = pl.BlockSpec(memory_space=pltpu.VMEM)
     hbm = pl.BlockSpec(memory_space=pltpu.HBM)
-    return pl.pallas_call(
+    received = pl.pallas_call(
         functools.partial(kernel, nz, n_leaf, chunks),
-        out_shape=jax.ShapeDtypeStruct(ancestor_tiles.shape, jnp.float32),
-        in_specs=[hbm] * 5,
-        out_specs=vmem,
+        out_shape=jax.ShapeDtypeStruct((n_leaf, tile_size, tile_size), jnp.float32),
+        in_specs=[hbm] * 3,
+        out_specs=hbm,
         scratch_shapes=[
             pltpu.VMEM((2 * rows, width), jnp.bfloat16),
             pltpu.VMEM(front_tiles.shape, jnp.float32),
-            pltpu.VMEM(ancestor_tiles.shape, jnp.float32),
             pltpu.SMEM(send_slots.shape, jnp.int32),
-            pltpu.SMEM(extend_slots.shape, jnp.int32),
             pltpu.VMEM((n_front, rows, width), jnp.bfloat16),
             pltpu.VMEM((blocks, tile_size, tile_size), jnp.float32),
             pltpu.VMEM((blocks, tile_size, tile_size), jnp.float32),
             pltpu.VMEM((blocks, tile_size, tile_size), jnp.float32),
             pltpu.VMEM((n_leaf, tile_size, tile_size), jnp.float32),
-            pltpu.VMEM((n_leaf, tile_size, tile_size), jnp.float32),
-            pltpu.SemaphoreType.DMA((5,)),
+            pltpu.SemaphoreType.DMA((3,)),
             pltpu.SemaphoreType.DMA((3, n_front, chunks)),
             pltpu.SemaphoreType.DMA((n_front, chunks)),
             pltpu.SemaphoreType.DMA((blocks, 2)),
@@ -360,7 +361,21 @@
             bytes_accessed=2 * n_front * rows * width,
             transcendentals=0,
         ),
-    )(factored_panel, front_tiles, ancestor_tiles, send_slots, extend_slots)
+    )(factored_panel, front_tiles, send_slots)
+    held = ancestor_tiles.shape[0]
+    group = held // 2 if held % 2 == 0 else held
+    part = pl.BlockSpec((group, tile_size, tile_size), lambda n: (n, 0, 0))
+    return pl.pallas_call(
+        extend_add,
+        grid=(held // group,),
+        out_shape=jax.ShapeDtypeStruct(ancestor_tiles.shape, jnp.float32),
+        in_specs=[
+            part,
+            pl.BlockSpec((n_leaf, tile_size, tile_size), lambda n: (0, 0, 0)),
+            pl.BlockSpec(memory_space=pltpu.SMEM),
+        ],
+        out_specs=part,
+    )(ancestor_tiles, received, extend_slots)
 
 
 def solution(mesh):

time: 36.6 us -> 35 us (0.956)
  local copies, waits for them, and re-layouts: 1.87 us -> 0 us
  Pallas kernels: 34.5 us -> 34.9 us
    pallas_call x0 -> x1, Pallas kernels: none -> 1.91 us  [shards(): pl.pallas_call(extend_add, grid=(held // group,), out_shape=jax.ShapeDtyp...]
    unnamed x1 -> x0, local copies, waits for them, and re-layouts: 1.87 us -> none
    pallas_call x1, Pallas kernels: 34.5 us -> 33 us  [shards(): pl.pallas_call(functools.partial(kernel, nz, n_leaf, chunks), out_shape=j...]
where the time goes in v3:
time: 35 us; the launch traced here: 34.9 us
  Pallas kernels  34.9 us (100%)
    pallas_call x1, Pallas kernels, shards(): pl.pallas_call(functools.partial(kernel, nz, n_leaf, chunks), out_shape=j...  33 us
    pallas_call x1, Pallas kernels, shards(): pl.pallas_call(extend_add, grid=(held // group,), out_shape=jax.ShapeDtyp...  1.91 us

profile of v3, /device:TPU:0, one launch (start us, length us, event | category | flops | bytes accessed | tf_op | source)
XLA Modules:
  0.0 34.9 jit_solution(17371097766748445105)
XLA Ops:
  0.0 33.0 %shard_map.55.received = f32[4,128,128]{2,1,0:T(8,128)} custom-call(bf16[128,1536]{1,0:T(8,128)(2,1)} %panel_hbm.1, f32[8,128,128]{2,1,0:T(8,128)} %front_hbm.1, s32[1,8]{1,0:T(1,128)} %targets_hbm.1), custom_call_target="tpu_custom_call" | custom-call | flops 402653184 | bytes 3145728 | tf_op jit(solution)/shard_map/pallas_call | solution.py:334
  33.0 1.9 %shard_map.56 = f32[8,128,128]{2,1,0:T(8,128)} custom-call(f32[8,128,128]{2,1,0:T(8,128)} %ancestor.1, f32[4,128,128]{2,1,0:T(8,128)} %shard_map.55.received, s32[1,4]{1,0:T(1,128)} %extend.1), custom_call_target="tpu_custom_call" | custom-call | tf_op jit(solution)/shard_map/pallas_call | solution.py:368

commit v4 on v3

--- a/solution.py
+++ b/solution.py
@@ -257,6 +257,18 @@
             pass_on(SIDE, panel, f, k).wait_send()
             pass_on(SIDE, panel, mate * 2 + c, k).wait_send()
 
+    loads[2].wait()
+
+    def find(d):
+        row, present = jnp.int32(0), jnp.int32(0)
+        for i in range(blocks):
+            hit = targets[0, i] == d
+            row = jnp.where(hit, i, row)
+            present = jnp.where(hit, 1, present)
+        return row, present
+
+    chosen = [find((leaf + j) % n_leaf) for j in range(n_leaf)]
+
     halves = nz == 4
     if halves:
         pl.when(inner)(inner_start)
@@ -264,14 +276,9 @@
     else:
         relay()
 
-    loads[2].wait()
-
-    def pick(d):
-        row, present = jnp.int32(0), jnp.int32(0)
-        for i in range(blocks):
-            hit = targets[0, i] == d
-            row = jnp.where(hit, i, row)
-            present = jnp.where(hit, 1, present)
+
+    def pick(j):
+        row, present = chosen[j]
         tile = schur[row]
         return jnp.where(present > 0, tile, jnp.zeros_like(tile))
 
@@ -286,9 +293,9 @@
         )
 
     for j in range(1, n_leaf):
-        message[j] = pick((leaf + j) % n_leaf)
+        message[j] = pick(j)
         leaf_copy(j).start()
-    message[0] = pick(leaf)
+    message[0] = pick(0)
     keep = pltpu.make_async_copy(message.at[0], received.at[leaf], leaf_recv.at[leaf])
     keep.start()
 

time: 35 us -> 35 us (level)
  no operation moved by 1% of the time
where the time goes in v4:
time: 35 us; the launch traced here: 34.9 us
  Pallas kernels  34.9 us (100%)
    pallas_call x1, Pallas kernels, shards(): pl.pallas_call(functools.partial(kernel, nz, n_leaf, chunks), out_shape=j...  33 us
    pallas_call x1, Pallas kernels, shards(): pl.pallas_call(extend_add, grid=(held // group,), out_shape=jax.ShapeDtyp...  1.91 us

profile of v4, /device:TPU:0, one launch (start us, length us, event | category | flops | bytes accessed | tf_op | source)
XLA Modules:
  0.0 34.9 jit_solution(5943930284168088257)
XLA Ops:
  0.0 33.0 %shard_map.55.received = f32[4,128,128]{2,1,0:T(8,128)} custom-call(bf16[128,1536]{1,0:T(8,128)(2,1)} %panel_hbm.1, f32[8,128,128]{2,1,0:T(8,128)} %front_hbm.1, s32[1,8]{1,0:T(1,128)} %targets_hbm.1), custom_call_target="tpu_custom_call" | custom-call | flops 402653184 | bytes 3145728 | tf_op jit(solution)/shard_map/pallas_call | solution.py:341
  33.0 1.9 %shard_map.56 = f32[8,128,128]{2,1,0:T(8,128)} custom-call(f32[8,128,128]{2,1,0:T(8,128)} %ancestor.1, f32[4,128,128]{2,1,0:T(8,128)} %shard_map.55.received, s32[1,4]{1,0:T(1,128)} %extend.1), custom_call_target="tpu_custom_call" | custom-call | tf_op jit(solution)/shard_map/pallas_call | solution.py:375
